TPU v7x, 32 devices: a whole 2x2x4 slice. The times are simulated.
32 devices in a mesh: segment: 2 (over x), tm: 4 (over z), space: 4 (over y, core).
Axes of the slice: x: 2, y: 2, z: 4, core: 2. Of those that a mesh axis runs over, the one named last changes fastest.
Arguments:
- clip_frames: bfloat16 [16, 32, 128, 128], P('tm', 'space'), may hold values from -6 to 6
- enc_weight: bfloat16 [3, 3, 3, 128, 256], replicated, may hold values from -0.109375 to 0.109375
- dec_weight: bfloat16 [3, 3, 3, 256, 128], replicated, may hold values from -0.078125 to 0.078125
- out_grad: bfloat16 [8, 16, 64, 128], P('tm', 'space'), may hold values from -6 to 6
Outputs:
- latent_pair: bfloat16 [2, 8, 16, 64, 256], P('segment', 'tm', 'space')
- weight_grads: float32 [2, 27, 32768], P('segment')
All inputs are finite; a program needn't handle non-finite values.
Results may differ from a plain program's by a relative error of at most 0.0056.
Values may be sent and summed in bfloat16 or wider, within the bound.
A program may use at most 128 MiB of HBM per device.

v0:
```python
import functools
import math

import jax
import jax.numpy as jnp
from jax import lax
from jax.experimental import pallas as pl
from jax.experimental.pallas import tpu as pltpu
from jax.sharding import PartitionSpec as P

MESH = pl.DeviceIdType.MESH
BF = jnp.bfloat16
F32 = jnp.float32
TAPS = 27
BLOCK = 3 * 256
CHUNKS = (
    ((2, 0),),
    ((2, 1), (2, 2)),
    ((0, 0), (0, 1)),
    ((0, 2), (1, 0)),
    ((1, 1),),
    ((1, 2),),
)


def mm(x, y):
    return jnp.dot(x, y, preferred_element_type=F32)


def kernel(
    T,
    S,
    shards,
    scale,
    clip,
    ew_h,
    dw_h,
    og_h,
    latp,
    wout,
    clipx,
    x3,
    ew,
    dw,
    og,
    pout,
    pin,
    ext,
    rim,
    s3,
    lg,
    gt,
    st,
    mix,
    part,
    rcv1,
    red1,
    rcvy,
    red2,
    rcvz,
    gat,
    lsem,
    ssem,
    rsem,
    c_sem,
    y_sem,
    z_sem,
    gz_sem,
    gy_sem,
    gc_sem,
    osem,
):
    seg = lax.axis_index("segment")
    k = lax.axis_index("tm")
    s = lax.axis_index("space")
    n = T * S
    Y = S // 2
    core = s % 2
    y = s // 2
    has_up, has_dn = s > 0, s < S - 1
    has_pv, has_nx = k > 0, k < T - 1
    is_enc = seg == 0

    loads = [
        pltpu.make_async_copy(clip, clipx.at[:, pl.ds(1, 8)], lsem.at[0]),
        pltpu.make_async_copy(ew_h, ew, lsem.at[1]),
        pltpu.make_async_copy(dw_h, dw, lsem.at[2]),
        pltpu.make_async_copy(og_h, og, lsem.at[3]),
    ]
    for c in loads:
        c.start()

    me = k * S + s
    barrier = pltpu.get_barrier_semaphore()

    def greet(d, carry):
        peer = (me + d) % n
        pl.semaphore_signal(
            barrier, inc=1, device_id=(seg, peer // S, peer % S), device_id_type=MESH
        )
        return carry

    lax.fori_loop(1, n, greet, 0)
    pl.semaphore_wait(barrier, n - 1)

    def remote(src, dst, i, to):
        return pltpu.make_async_remote_copy(
            src_ref=src,
            dst_ref=dst,
            send_sem=ssem.at[i],
            recv_sem=rsem.at[i],
            device_id=to,
            device_id_type=MESH,
        )

    def launch(entries):
        for copy, sends, gets, dst in entries:

            @pl.when(sends)
            def _():
                copy.start()

    def collect(entries):
        for copy, sends, gets, dst in entries:

            @pl.when(gets)
            def _():
                copy.wait_recv()

            @pl.when(jnp.logical_not(gets))
            def _():
                dst[...] = jnp.zeros(dst.shape, dst.dtype)

    def drain(entries):
        for copy, sends, gets, dst in entries:

            @pl.when(sends)
            def _():
                copy.wait_send()

    def entry(src, there, i, to, sends, gets):
        return (remote(src, there, i, to), sends, gets, there)

    e_clip = [
        entry(clip.at[:, pl.ds(7, 1)], clipx.at[:, pl.ds(0, 1)], 0, (seg, k, s + 1), has_dn, has_up)
    ]
    launch(e_clip)

    sel_i = lax.broadcasted_iota(jnp.int32, (192, 128), 0)
    sel_j = lax.broadcasted_iota(jnp.int32, (192, 128), 1)
    sel = (sel_j == 2 * (sel_i % 64) + sel_i // 64 - 1).astype(F32).astype(BF)

    def split_cols(f, r):
        y = mm(sel, clipx[f, r]).astype(BF)
        x3[f, r] = jnp.concatenate([y[:64], y[64:128], y[128:]], axis=1)

    loads[0].wait()

    def split_frame(f, carry):
        for r in range(1, 9):
            split_cols(f, r)
        return carry

    lax.fori_loop(0, 4, split_frame, 0)
    collect(e_clip)
    for f in range(4):
        split_cols(f, 0)
    loads[1].wait()

    def xrows(f, b):
        return jnp.concatenate([x3[f, b + 2 * h] for h in range(4)], axis=0)

    acc = jnp.zeros((256, 256), F32)
    for a in range(2):
        for b in range(3):
            acc = acc + mm(xrows(2 + a, b), ew[3 * a + b])
    pout[...] = acc.astype(BF)
    e_part = [entry(pout, pin, 1, (seg, k + 1, s), has_nx, has_pv)]
    launch(e_part)

    def lat_entries(f, base):
        own = 2 + f
        return [
            entry(ext.at[own, pl.ds(1, 4)], ext.at[f, pl.ds(1, 4)], base, (seg, k + 1, s), has_nx, has_pv),
            entry(ext.at[own, pl.ds(4, 1)], ext.at[own, pl.ds(0, 1)], base + 1, (seg, k, s + 1), has_dn, has_up),
            entry(ext.at[own, pl.ds(1, 1)], ext.at[own, pl.ds(5, 1)], base + 2, (seg, k, s - 1), has_up, has_dn),
            entry(
                ext.at[own, pl.ds(4, 1)],
                ext.at[f, pl.ds(0, 1)],
                base + 3,
                (seg, k + 1, s + 1),
                has_nx & has_dn,
                has_pv & has_up,
            ),
            entry(
                ext.at[own, pl.ds(1, 1)],
                ext.at[f, pl.ds(5, 1)],
                base + 4,
                (seg, k + 1, s - 1),
                has_nx & has_up,
                has_pv & has_dn,
            ),
        ]

    acc = jnp.zeros((256, 256), F32)
    for a in range(3):
        for b in range(3):
            acc = acc + mm(xrows(a, b), ew[3 * a + b])
    ext[3, 1:5] = acc.astype(BF).reshape(4, 64, 256)
    e_lat1 = lat_entries(1, 2)
    launch(e_lat1)

    acc = jnp.zeros((256, 256), F32)
    for b in range(3):
        acc = acc + mm(xrows(0, b), ew[6 + b])
    collect(e_part)
    ext[2, 1:5] = (acc + pin[...].astype(F32)).astype(BF).reshape(4, 64, 256)
    e_lat0 = lat_entries(0, 7)
    launch(e_lat0)

    loads[2].wait()
    loads[3].wait()
    col = lax.broadcasted_iota(jnp.int32, (256, 128), 0) % 64

    def dcat(ab):
        return jnp.concatenate([dw[3 * ab], dw[3 * ab + 1], dw[3 * ab + 2]], axis=1)

    def erows(f, b):
        return jnp.concatenate([ext[f, b + h] for h in range(4)], axis=0)

    def decode(acc, t, taps_t):
        for a in taps_t:
            for b in range(3):
                acc = acc + mm(erows(t + a, b), dcat(3 * a + b))
        return acc

    def slope_of(acc, t):
        before = jnp.where(col == 0, 0.0, pltpu.roll(acc[:, :128], 1, 0))
        after = jnp.where(col == 63, 0.0, pltpu.roll(acc[:, 256:], 255, 0))
        pre = before + acc[:, 128:256] + after
        sg = jax.nn.sigmoid(pre)
        slope = og[t].reshape(256, 128).astype(F32) * sg * (1.0 + pre * (1.0 - sg))
        rim[t, 1:5] = slope.astype(BF).reshape(4, 64, 128)

    def slope_entries(f, base):
        own = rim.at[f, pl.ds(1, 4)]
        top = rim.at[f, pl.ds(1, 1)]
        last = rim.at[f, pl.ds(4, 1)]
        far = 2 + f
        return [
            entry(own, rim.at[far, pl.ds(1, 4)], base, (seg, k - 1, s), has_pv, has_nx),
            entry(last, rim.at[f, pl.ds(0, 1)], base + 1, (seg, k, s + 1), has_dn, has_up),
            entry(top, rim.at[f, pl.ds(5, 1)], base + 2, (seg, k, s - 1), has_up, has_dn),
            entry(last, rim.at[far, pl.ds(0, 1)], base + 3, (seg, k - 1, s + 1), has_pv & has_dn, has_nx & has_up),
            entry(top, rim.at[far, pl.ds(5, 1)], base + 4, (seg, k - 1, s - 1), has_pv & has_up, has_nx & has_dn),
        ]

    e_slope1 = slope_entries(1, 12)
    e_slope0 = slope_entries(0, 17)
    e_lg = [entry(lg.at[0], lg.at[2], 22, (seg, k - 1, s), has_pv, has_nx)]

    collect(e_lat1[1:3])
    collect(e_lat0[1:3])
    zero = jnp.zeros((256, 384), F32)
    acc1 = decode(zero, 1, (1, 2))
    acc0 = decode(zero, 0, (2,))
    collect(e_lat1[:1] + e_lat1[3:])
    slope_of(decode(acc1, 1, (0,)), 1)

    @pl.when(is_enc)
    def _():
        launch(e_slope1)

    acc0 = decode(acc0, 0, (1,))
    collect(e_lat0[:1] + e_lat0[3:])
    slope_of(decode(acc0, 0, (0,)), 0)

    @pl.when(is_enc)
    def _():
        launch(e_slope0)

    col64 = lax.broadcasted_iota(jnp.int32, (64, 128), 0)

    def shifts(v):
        later = jnp.where(col64 == 63, 0.0, pltpu.roll(v, 63, 0))
        sooner = jnp.where(col64 == 0, 0.0, pltpu.roll(v, 1, 0))
        return jnp.concatenate([later, v, sooner], axis=1)

    def put_shifts(f, which):
        for r in which:
            s3[f, r] = shifts(rim[f, r].astype(F32)).astype(BF)

    def transpose(acc, t, taps_t):
        for a in taps_t:
            for b in range(3):
                cells = jnp.concatenate([s3[t + 2 - a, h + 2 - b] for h in range(4)], axis=0)
                acc = acc + lax.dot_general(
                    cells, dcat(3 * a + b), (((1,), (1,)), ((), ())), preferred_element_type=F32
                )
        return acc

    def keep(acc, t):
        rounded = acc.astype(BF)
        lg[t] = rounded.reshape(4, 64, 256)
        if t == 0:
            launch(e_lg)
        gt[:, t * 256 : (t + 1) * 256] = rounded.astype(F32).T.astype(BF)

    @pl.when(is_enc)
    def _():
        for f in (1, 0):
            put_shifts(f, range(1, 5))
        collect(e_slope1[1:3])
        collect(e_slope0[1:3])
        for f in (1, 0):
            put_shifts(f, (0, 5))
        zero = jnp.zeros((256, 256), F32)
        acc0 = transpose(zero, 0, (1, 2))
        acc1 = transpose(zero, 1, (2,))
        collect(e_slope1[:1] + e_slope1[3:])
        put_shifts(3, range(6))
        collect(e_slope0[:1] + e_slope0[3:])
        put_shifts(2, range(6))
        keep(transpose(acc0, 0, (0,)), 0)
        keep(transpose(acc1, 1, (0, 1)), 1)
        pltpu.make_async_copy(lg.at[pl.ds(0, 2)], latp, osem.at[0]).start()

    @pl.when(jnp.logical_not(is_enc))
    def _():
        pltpu.make_async_copy(ext.at[pl.ds(2, 2), pl.ds(1, 4)], latp, osem.at[0]).start()
        for t in range(2):
            cells = jnp.concatenate([shifts(rim[t, 1 + h].astype(F32)) for h in range(4)], axis=0)
            st[:, t * 256 : (t + 1) * 256] = cells.T.astype(BF)

    def enc_block(a, b, at):
        frames, lanes = (1, 3) if a == 1 else (0, 2), 0 if a == 2 else 256
        cells = jnp.concatenate([xrows(f, b) for f in frames], axis=0)
        grad = mm(gt[:, lanes : lanes + 512], cells)
        for c in range(3):
            whole = grad[:, c * 128 : (c + 1) * 128].T
            mix[c, pl.ds(0, 128, stride=2), :] = whole[:, :128]
            mix[c, pl.ds(1, 128, stride=2), :] = whole[:, 128:]
            part[at + c * 256 : at + (c + 1) * 256, :] = mix[c].astype(BF)

    def dec_block(a, b, at):
        cells = jnp.concatenate([erows(a, b), erows(1 + a, b)], axis=0)
        grad = mm(st[...], cells)
        for c in range(3):
            part[at + c * 256 : at + (c + 1) * 256, :] = grad[c * 128 : (c + 1) * 128].T.astype(BF)

    sh = shards
    off = [sum(sh[:j]) for j in range(len(sh))]

    def grads(j):
        at = off[j] * n

        @pl.when(is_enc)
        def _():
            if CHUNKS[j][0] == (0, 0):
                collect(e_lg)
                gt[:, 512:768] = lg[2].reshape(256, 256).astype(F32).T.astype(BF)
            for i, (a, b) in enumerate(CHUNKS[j]):
                enc_block(a, b, at + i * BLOCK)

        @pl.when(jnp.logical_not(is_enc))
        def _():
            for i, (a, b) in enumerate(CHUNKS[j]):
                dec_block(a, b, at + i * BLOCK)

        used = BLOCK * len(CHUNKS[j])
        if n * sh[j] > used:
            part[at + used : at + n * sh[j], :] = jnp.zeros((n * sh[j] - used, 128), BF)

    def rows(start, count):
        return pl.ds(pl.multiple_of(start, 16), count)

    def move(src, dst, sems, i, to):
        return pltpu.make_async_remote_copy(
            src_ref=src,
            dst_ref=dst,
            send_sem=sems.at[0, i],
            recv_sem=sems.at[1, i],
            device_id=to,
            device_id_type=MESH,
        )

    sibling = (seg, k, s + 1 - 2 * core)
    sent = []

    def send(copy):
        copy.start()
        sent.append(copy)

    def arrived(dst, sems, i):
        move(dst, dst, sems, i, sibling).wait_recv()

    def at_y(p):
        return (seg, k, 2 * p + core)

    def half_of(ref, j):
        return ref.at[off[j] * n // 2 : off[j] * n // 2 + sh[j] * n // 2]

    def core_start(j):
        away = part.at[rows(off[j] * n + (1 - core) * (sh[j] * n // 2), sh[j] * n // 2)]
        send(move(away, half_of(rcv1, j), c_sem, j, sibling))

    def y_start(j):
        count = sh[j] * n // 2
        lo = off[j] * n // 2
        arrived(half_of(rcv1, j), c_sem, j)
        own = part[rows(off[j] * n + core * count, count), :].astype(F32)
        red1[lo : lo + count, :] = (own + rcv1[lo : lo + count, :].astype(F32)).astype(BF)
        for d in range(1, Y):
            p = (y + d) % Y
            i = j * (Y - 1) + d - 1
            slot = rcvy.at[d - 1, off[j] * T : (off[j] + sh[j]) * T]
            send(move(red1.at[rows(lo + p * T * sh[j], T * sh[j])], slot, y_sem, i, at_y(p)))

    def z_start(j):
        lo, count = off[j] * T, sh[j] * T
        total = red1[rows(off[j] * n // 2 + y * count, count), :].astype(F32)
        for d in range(1, Y):
            arrived(rcvy.at[d - 1, lo : lo + count], y_sem, j * (Y - 1) + d - 1)
            total = total + rcvy[d - 1, lo : lo + count, :].astype(F32)
        red2[lo : lo + count, :] = total.astype(BF)
        for d in range(1, T):
            p = (k + d) % T
            i = j * (T - 1) + d - 1
            slot = rcvz.at[d - 1, off[j] : off[j] + sh[j]]
            send(move(red2.at[rows(lo + p * sh[j], sh[j])], slot, z_sem, i, (seg, p, s)))

    def shard(j, py, pz):
        return rows(off[j] * n + ((core * Y + py) * T + pz) * sh[j], sh[j])

    def band(j, pc, py):
        return gat.at[rows(off[j] * n + (pc * Y + py) * T * sh[j], T * sh[j])]

    def gz_start(j):
        total = red2[rows(off[j] * T + k * sh[j], sh[j]), :].astype(F32)
        for d in range(1, T):
            arrived(rcvz.at[d - 1, off[j] : off[j] + sh[j]], z_sem, j * (T - 1) + d - 1)
            total = total + rcvz[d - 1, off[j] : off[j] + sh[j], :].astype(F32)
        mine = shard(j, y, k)
        gat[mine, :] = (total * scale).astype(BF)
        for d in range(1, T):
            send(move(gat.at[mine], gat.at[mine], gz_sem, j * (T - 1) + d - 1, (seg, (k + d) % T, s)))

    def gy_start(j):
        for d in range(1, T):
            arrived(gat.at[shard(j, y, (k - d + T) % T)], gz_sem, j * (T - 1) + d - 1)
        mine = band(j, core, y)
        for d in range(1, Y):
            send(move(mine, mine, gy_sem, j * (Y - 1) + d - 1, at_y((y + d) % Y)))
        send(move(mine, mine, gc_sem, j * Y, sibling))

    def gc_start(j):
        for d in range(1, Y):
            theirs = band(j, core, (y - d + Y) % Y)
            arrived(theirs, gy_sem, j * (Y - 1) + d - 1)
            send(move(theirs, theirs, gc_sem, j * Y + d, sibling))

    def written(j):
        copies = []
        for i, (a, b) in enumerate(CHUNKS[j]):
            src = gat.at[off[j] * n + i * BLOCK : off[j] * n + (i + 1) * BLOCK]
            dst = wout.at[(3 * a + b) * BLOCK : (3 * a + b + 1) * BLOCK]
            copies.append(pltpu.make_async_copy(src, dst, osem.at[1 + 3 * a + b]))
        return copies

    def finish(j):
        for d in range(Y):
            arrived(band(j, 1 - core, (y - d + Y) % Y), gc_sem, j * Y + d)
        for copy in written(j):
            copy.start()

    stages = [y_start, z_start, gz_start, gy_start, gc_start, finish]
    count = len(CHUNKS)
    for step in range(count + len(stages)):
        if step < count:
            grads(step)
            core_start(step)
        for j in range(count):
            if 0 <= step - j - 1 < len(stages):
                stages[step - j - 1](j)

    for copy in sent:
        copy.wait_send()

    @pl.when(is_enc)
    def _():
        drain(e_slope1)
        drain(e_slope0)
        drain(e_lg)

    drain(e_clip)
    drain(e_part)
    drain(e_lat1)
    drain(e_lat0)
    pltpu.make_async_copy(lg.at[pl.ds(0, 2)], latp, osem.at[0]).wait()
    for j in range(count):
        for copy in written(j):
            copy.wait()


def solution(mesh):
    T, S = mesh.shape["tm"], mesh.shape["space"]
    n = T * S
    shards = tuple(-(-len(blocks) * BLOCK // n // 16) * 16 for blocks in CHUNKS)
    sh = sum(shards)
    Y = S // 2
    half = n // 2 * sh
    count = len(CHUNKS)

    def on_device(clip_frames, enc_weight, dec_weight, out_grad):
        scale = 1.0 / math.sqrt(2 * 4 * 64 * n)
        dma = pltpu.SemaphoreType.DMA
        latp, wout = pl.pallas_call(
            functools.partial(kernel, T, S, shards, scale),
            out_shape=(
                jax.ShapeDtypeStruct((2, 4, 64, 256), BF),
                jax.ShapeDtypeStruct((9 * BLOCK, 128), BF),
            ),
            in_specs=[pl.BlockSpec(memory_space=pltpu.HBM)] * 4,
            out_specs=(pl.BlockSpec(memory_space=pl.ANY),) * 2,
            scratch_shapes=[
                pltpu.VMEM((4, 9, 128, 128), BF),
                pltpu.VMEM((4, 9, 64, 384), BF),
                pltpu.VMEM((9, 384, 256), BF),
                pltpu.VMEM((27, 256, 128), BF),
                pltpu.VMEM((2, 4, 64, 128), BF),
                pltpu.VMEM((256, 256), BF),
                pltpu.VMEM((256, 256), BF),
                pltpu.VMEM((4, 6, 64, 256), BF),
                pltpu.VMEM((4, 6, 64, 128), BF),
                pltpu.VMEM((4, 6, 64, 384), BF),
                pltpu.VMEM((3, 4, 64, 256), BF),
                pltpu.VMEM((256, 768), BF),
                pltpu.VMEM((384, 512), BF),
                pltpu.VMEM((3, 256, 128), F32),
                pltpu.VMEM((n * sh, 128), BF),
                pltpu.VMEM((half, 128), BF),
                pltpu.VMEM((half, 128), BF),
                pltpu.VMEM((Y - 1, T * sh, 128), BF),
                pltpu.VMEM((T * sh, 128), BF),
                pltpu.VMEM((T - 1, sh, 128), BF),
                pltpu.VMEM((n * sh, 128), BF),
                dma((4,)),
                dma((23,)),
                dma((23,)),
                dma((2, count)),
                dma((2, count * (Y - 1))),
                dma((2, count * (T - 1))),
                dma((2, count * (T - 1))),
                dma((2, count * (Y - 1))),
                dma((2, count * Y)),
                dma((10,)),
            ],
            compiler_params=pltpu.CompilerParams(
                collective_id=0, has_side_effects=True, vmem_limit_bytes=60 * 1024 * 1024
            ),
            cost_estimate=pl.CostEstimate(
                flops=5 * 10**9, bytes_accessed=12 * 10**6, transcendentals=65536
            ),
        )(
            clip_frames,
            enc_weight.reshape(9, 384, 256),
            dec_weight.reshape(27, 256, 128),
            out_grad,
        )
        flat = wout.reshape(1, TAPS, 32768).astype(F32)
        return latp[None], flat

    placed = (P("tm", "space", None, None), P(), P(), P("tm", "space", None, None))
    return jax.shard_map(
        on_device,
        mesh=mesh,
        in_specs=placed,
        out_specs=(P("segment", "tm", "space", None, None), P("segment", None, None)),
        check_vma=False,
    )
```

profile of v0, /device:TPU:1, one launch (start us, length us, event | category | flops | bytes accessed | tf_op | source)
XLA Modules:
  0.0 74.3 jit_solution(5553944196892750993)
XLA Ops:
  0.6 69.4 %shard_map.59 = (bf16[2,4,64,256]{3,2,1,0:T(8,128)(2,1)}, bf16[6912,128]{1,0:T(8,128)(2,1)}) custom-call(bf16[4,8,128,128]{3,2,1,0:T(8,128)(2,1)} %clip.1, bf16[9,384,256]{2,1,0:T(8,128)(2,1)} %bitcast.6, bf16[27,256,128]{2,1,0:T(8,128)(2,1)} %bitcast.7, bf16[2,4,64,128]{3,2,1,0:T(8,128)(2,1)} %og_h.1), custom_call_target="tpu_custom_call" | custom-call | flops 5000000000 | bytes 12000000 | tf_op jit(solution)/shard_map/pallas_call | solution.py:517
  70.0 0.0 copy-start
  70.0 3.5 %convert_element_type.16 = f32[6912,128]{1,0:T(8,128)} convert(bf16[6912,128]{1,0:T(8,128)(2,1)} %get-tuple-element.5) | non-fusion elementwise | flops 884736 | bytes 5308416 | tf_op jit(solution)/shard_map/convert_element_type | solution.py:570
  73.6 0.0 copy-done
  73.6 0.7 copy.9
Async XLA Ops:
  70.0 3.6 %copy-start = (bf16[2,4,64,256]{3,2,1,0:T(8,128)(2,1)S(1)}, bf16[2,4,64,256]{3,2,1,0:T(8,128)(2,1)}, u32[]{:S(2)}) copy-start(bf16[2,4,64,256]{3,2,1,0:T(8,128)(2,1)} %get-tuple-element.4) | copy-start | bytes 786436
where the time goes:
time: 74.4 us; the launch traced here: 74.3 us
  Pallas kernels  69.4 us (93%)
  other arithmetic  3.54 us (5%)
    pallas_call x1, Pallas kernels, on_device(): pl.pallas_call(functools.partial(kernel, T, S, shards, scale), out_shape=...  69.4 us
    convert_element_type x1, other arithmetic, on_device(): flat = wout.reshape(1, TAPS, 32768).astype(F32)  3.54 us

commit v1 on v0

--- a/solution.py
+++ b/solution.py
@@ -14,12 +14,9 @@
 TAPS = 27
 BLOCK = 3 * 256
 CHUNKS = (
-    ((2, 0),),
-    ((2, 1), (2, 2)),
-    ((0, 0), (0, 1)),
-    ((0, 2), (1, 0)),
-    ((1, 1),),
-    ((1, 2),),
+    ((2, 0), (2, 1), (2, 2)),
+    ((0, 0), (0, 1), (0, 2)),
+    ((1, 0), (1, 1), (1, 2)),
 )
 
 
@@ -42,6 +39,7 @@
     x3,
     ew,
     dw,
+    dwt,
     og,
     pout,
     pin,
@@ -213,13 +211,27 @@
     acc = jnp.zeros((256, 256), F32)
     for b in range(3):
         acc = acc + mm(xrows(0, b), ew[6 + b])
+    loads[2].wait()
+    loads[3].wait()
+
+    def turn(ab, carry):
+        for c in range(3):
+            dwt[ab, c * 128 : (c + 1) * 128, :] = dw[3 * ab + c].astype(F32).T.astype(BF)
+        return carry
+
+    @pl.when(is_enc)
+    def _():
+        lax.fori_loop(0, 4, turn, 0)
+
     collect(e_part)
     ext[2, 1:5] = (acc + pin[...].astype(F32)).astype(BF).reshape(4, 64, 256)
     e_lat0 = lat_entries(0, 7)
     launch(e_lat0)
 
-    loads[2].wait()
-    loads[3].wait()
+    @pl.when(is_enc)
+    def _():
+        lax.fori_loop(4, 9, turn, 0)
+
     col = lax.broadcasted_iota(jnp.int32, (256, 128), 0) % 64
 
     def dcat(ab):
@@ -294,9 +306,7 @@
         for a in taps_t:
             for b in range(3):
                 cells = jnp.concatenate([s3[t + 2 - a, h + 2 - b] for h in range(4)], axis=0)
-                acc = acc + lax.dot_general(
-                    cells, dcat(3 * a + b), (((1,), (1,)), ((), ())), preferred_element_type=F32
-                )
+                acc = acc + mm(cells, dwt[3 * a + b])
         return acc
 
     def keep(acc, t):
@@ -527,6 +537,7 @@
                 pltpu.VMEM((4, 9, 64, 384), BF),
                 pltpu.VMEM((9, 384, 256), BF),
                 pltpu.VMEM((27, 256, 128), BF),
+                pltpu.VMEM((9, 384, 256), BF),
                 pltpu.VMEM((2, 4, 64, 128), BF),
                 pltpu.VMEM((256, 256), BF),
                 pltpu.VMEM((256, 256), BF),

time: 74.4 us -> 71.8 us (0.965)
  Pallas kernels: 69.4 us -> 66.8 us
    pallas_call x1, Pallas kernels: 69.4 us -> 66.8 us  [on_device(): pl.pallas_call(functools.partial(kernel, T, S, shards, scale), out_shape=...]
where the time goes in v1:
time: 71.8 us; the launch traced here: 71.7 us
  Pallas kernels  66.8 us (93%)
  other arithmetic  3.54 us (5%)
    pallas_call x1, Pallas kernels, on_device(): pl.pallas_call(functools.partial(kernel, T, S, shards, scale), out_shape=...  66.8 us
    convert_element_type x1, other arithmetic, on_device(): flat = wout.reshape(1, TAPS, 32768).astype(F32)  3.54 us

profile of v1, /device:TPU:1, one launch (start us, length us, event | category | flops | bytes accessed | tf_op | source)
XLA Modules:
  0.0 71.7 jit_solution(6034114424401632289)
XLA Ops:
  0.6 66.8 %shard_map.59 = (bf16[2,4,64,256]{3,2,1,0:T(8,128)(2,1)}, bf16[6912,128]{1,0:T(8,128)(2,1)}) custom-call(bf16[4,8,128,128]{3,2,1,0:T(8,128)(2,1)} %clip.1, bf16[9,384,256]{2,1,0:T(8,128)(2,1)} %bitcast.6, bf16[27,256,128]{2,1,0:T(8,128)(2,1)} %bitcast.7, bf16[2,4,64,128]{3,2,1,0:T(8,128)(2,1)} %og_h.1), custom_call_target="tpu_custom_call" | custom-call | flops 5000000000 | bytes 12000000 | tf_op jit(solution)/shard_map/pallas_call | solution.py:527
  67.4 0.0 copy-start
  67.4 3.5 %convert_element_type.16 = f32[6912,128]{1,0:T(8,128)} convert(bf16[6912,128]{1,0:T(8,128)(2,1)} %get-tuple-element.5) | non-fusion elementwise | flops 884736 | bytes 5308416 | tf_op jit(solution)/shard_map/convert_element_type | solution.py:581
  70.9 0.0 copy-done
  70.9 0.7 copy.9
Async XLA Ops:
  67.4 3.6 %copy-start = (bf16[2,4,64,256]{3,2,1,0:T(8,128)(2,1)S(1)}, bf16[2,4,64,256]{3,2,1,0:T(8,128)(2,1)}, u32[]{:S(2)}) copy-start(bf16[2,4,64,256]{3,2,1,0:T(8,128)(2,1)} %get-tuple-element.4) | copy-start | bytes 786436

commit v2 on v1

--- a/solution.py
+++ b/solution.py
@@ -22,6 +22,10 @@
 
 def mm(x, y):
     return jnp.dot(x, y, preferred_element_type=F32)
+
+
+def widen(narrow, wide):
+    wide[...] = narrow[...].astype(F32)
 
 
 def kernel(
@@ -80,13 +84,14 @@
     is_enc = seg == 0
 
     loads = [
-        pltpu.make_async_copy(clip, clipx.at[:, pl.ds(1, 8)], lsem.at[0]),
+        pltpu.make_async_copy(clip.at[pl.ds(2, 2)], clipx.at[pl.ds(2, 2), pl.ds(1, 8)], lsem.at[0]),
         pltpu.make_async_copy(ew_h, ew, lsem.at[1]),
         pltpu.make_async_copy(dw_h, dw, lsem.at[2]),
         pltpu.make_async_copy(og_h, og, lsem.at[3]),
+        pltpu.make_async_copy(clip.at[pl.ds(0, 2)], clipx.at[pl.ds(0, 2), pl.ds(1, 8)], lsem.at[4]),
     ]
-    for c in loads:
-        c.start()
+    for i in (0, 1, 4, 2, 3):
+        loads[i].start()
 
     me = k * S + s
     barrier = pltpu.get_barrier_semaphore()
@@ -139,9 +144,11 @@
     def entry(src, there, i, to, sends, gets):
         return (remote(src, there, i, to), sends, gets, there)
 
-    e_clip = [
-        entry(clip.at[:, pl.ds(7, 1)], clipx.at[:, pl.ds(0, 1)], 0, (seg, k, s + 1), has_dn, has_up)
-    ]
+    def clip_entry(f, i):
+        src = clip.at[pl.ds(f, 2), pl.ds(7, 1)]
+        return entry(src, clipx.at[pl.ds(f, 2), pl.ds(0, 1)], i, (seg, k, s + 1), has_dn, has_up)
+
+    e_clip = [clip_entry(2, 0), clip_entry(0, 23)]
     launch(e_clip)
 
     sel_i = lax.broadcasted_iota(jnp.int32, (192, 128), 0)
@@ -151,17 +158,16 @@
     def split_cols(f, r):
         y = mm(sel, clipx[f, r]).astype(BF)
         x3[f, r] = jnp.concatenate([y[:64], y[64:128], y[128:]], axis=1)
-
-    loads[0].wait()
 
     def split_frame(f, carry):
         for r in range(1, 9):
             split_cols(f, r)
         return carry
 
-    lax.fori_loop(0, 4, split_frame, 0)
-    collect(e_clip)
-    for f in range(4):
+    loads[0].wait()
+    lax.fori_loop(2, 4, split_frame, 0)
+    collect(e_clip[:1])
+    for f in range(2, 4):
         split_cols(f, 0)
     loads[1].wait()
 
@@ -175,6 +181,11 @@
     pout[...] = acc.astype(BF)
     e_part = [entry(pout, pin, 1, (seg, k + 1, s), has_nx, has_pv)]
     launch(e_part)
+    loads[4].wait()
+    lax.fori_loop(0, 2, split_frame, 0)
+    collect(e_clip[1:])
+    for f in range(2):
+        split_cols(f, 0)
 
     def lat_entries(f, base):
         own = 2 + f
@@ -555,9 +566,9 @@
                 pltpu.VMEM((T * sh, 128), BF),
                 pltpu.VMEM((T - 1, sh, 128), BF),
                 pltpu.VMEM((n * sh, 128), BF),
-                dma((4,)),
-                dma((23,)),
-                dma((23,)),
+                dma((5,)),
+                dma((24,)),
+                dma((24,)),
                 dma((2, count)),
                 dma((2, count * (Y - 1))),
                 dma((2, count * (T - 1))),
@@ -578,8 +589,15 @@
             dec_weight.reshape(27, 256, 128),
             out_grad,
         )
-        flat = wout.reshape(1, TAPS, 32768).astype(F32)
-        return latp[None], flat
+        wide = pl.pallas_call(
+            widen,
+            grid=(6,),
+            out_shape=jax.ShapeDtypeStruct((9 * BLOCK, 128), F32),
+            in_specs=[pl.BlockSpec((9 * BLOCK // 6, 128), lambda i: (i, 0))],
+            out_specs=pl.BlockSpec((9 * BLOCK // 6, 128), lambda i: (i, 0)),
+            cost_estimate=pl.CostEstimate(flops=0, bytes_accessed=54 * BLOCK * 128, transcendentals=0),
+        )(wout)
+        return latp[None], wide.reshape(1, TAPS, 32768)
 
     placed = (P("tm", "space", None, None), P(), P(), P("tm", "space", None, None))
     return jax.shard_map(

time: 71.8 us -> 70.9 us (0.987)
  other arithmetic: 3.54 us -> 0 us
  Pallas kernels: 66.8 us -> 69.2 us
    pallas_call x0 -> x1, Pallas kernels: none -> 4.94 us  [on_device(): pl.pallas_call(widen, grid=(6,), out_shape=jax.ShapeDtypeStruct((9 * BLOC...]
    convert_element_type x1 -> x0, other arithmetic: 3.54 us -> none  [on_device(): flat = wout.reshape(1, TAPS, 32768).astype(F32)]
    pallas_call x1, Pallas kernels: 66.8 us -> 64.2 us  [on_device(): pl.pallas_call(functools.partial(kernel, T, S, shards, scale), out_shape=...]
where the time goes in v2:
time: 70.9 us; the launch traced here: 70.5 us
  Pallas kernels  69.2 us (98%)
  local copies, waits for them, and re-layouts  0.71 us (1%)
    pallas_call x1, Pallas kernels, on_device(): pl.pallas_call(functools.partial(kernel, T, S, shards, scale), out_shape=...  64.2 us
    pallas_call x1, Pallas kernels, on_device(): pl.pallas_call(widen, grid=(6,), out_shape=jax.ShapeDtypeStruct((9 * BLOC...  4.94 us

profile of v2, /device:TPU:1, one launch (start us, length us, event | category | flops | bytes accessed | tf_op | source)
XLA Modules:
  0.0 70.5 jit_solution(15210812184566526544)
XLA Ops:
  0.6 64.2 %shard_map.59 = (bf16[2,4,64,256]{3,2,1,0:T(8,128)(2,1)}, bf16[6912,128]{1,0:T(8,128)(2,1)}) custom-call(bf16[4,8,128,128]{3,2,1,0:T(8,128)(2,1)} %clip.1, bf16[9,384,256]{2,1,0:T(8,128)(2,1)} %bitcast.6, bf16[27,256,128]{2,1,0:T(8,128)(2,1)} %bitcast.7, bf16[2,4,64,128]{3,2,1,0:T(8,128)(2,1)} %og_h.1), custom_call_target="tpu_custom_call" | custom-call | flops 5000000000 | bytes 12000000 | tf_op jit(solution)/shard_map/pallas_call | solution.py:538
  64.9 0.0 copy-start
  64.9 4.9 %shard_map.60 = f32[6912,128]{1,0:T(8,128)} custom-call(bf16[6912,128]{1,0:T(8,128)(2,1)} %get-tuple-element.5.narrow), custom_call_target="tpu_custom_call" | custom-call | bytes 5308416 | tf_op jit(solution)/shard_map/pallas_call | solution.py:592
  69.8 0.0 copy-done
  69.8 0.7 copy.9
Async XLA Ops:
  64.9 4.9 %copy-start = (bf16[2,4,64,256]{3,2,1,0:T(8,128)(2,1)S(1)}, bf16[2,4,64,256]{3,2,1,0:T(8,128)(2,1)}, u32[]{:S(2)}) copy-start(bf16[2,4,64,256]{3,2,1,0:T(8,128)(2,1)} %get-tuple-element.4) | copy-start | bytes 786436

commit v3 on v2

--- a/solution.py
+++ b/solution.py
@@ -22,10 +22,6 @@
 
 def mm(x, y):
     return jnp.dot(x, y, preferred_element_type=F32)
-
-
-def widen(narrow, wide):
-    wide[...] = narrow[...].astype(F32)
 
 
 def kernel(
@@ -70,6 +66,7 @@
     gz_sem,
     gy_sem,
     gc_sem,
+    gl_sem,
     osem,
 ):
     seg = lax.axis_index("segment")
@@ -166,18 +163,20 @@
 
     loads[0].wait()
     lax.fori_loop(2, 4, split_frame, 0)
+    loads[1].wait()
+
+    def xrows(f, b):
+        return jnp.concatenate([x3[f, b + 2 * h] for h in range(4)], axis=0)
+
+    acc = jnp.zeros((256, 256), F32)
+    for a in range(2):
+        for b in (1, 2):
+            acc = acc + mm(xrows(2 + a, b), ew[3 * a + b])
     collect(e_clip[:1])
     for f in range(2, 4):
         split_cols(f, 0)
-    loads[1].wait()
-
-    def xrows(f, b):
-        return jnp.concatenate([x3[f, b + 2 * h] for h in range(4)], axis=0)
-
-    acc = jnp.zeros((256, 256), F32)
     for a in range(2):
-        for b in range(3):
-            acc = acc + mm(xrows(2 + a, b), ew[3 * a + b])
+        acc = acc + mm(xrows(2 + a, 0), ew[3 * a])
     pout[...] = acc.astype(BF)
     e_part = [entry(pout, pin, 1, (seg, k + 1, s), has_nx, has_pv)]
     launch(e_part)
@@ -418,6 +417,8 @@
     def at_y(p):
         return (seg, k, 2 * p + core)
 
+    last = len(CHUNKS) - 1
+
     def half_of(ref, j):
         return ref.at[off[j] * n // 2 : off[j] * n // 2 + sh[j] * n // 2]
 
@@ -465,19 +466,29 @@
         gat[mine, :] = (total * scale).astype(BF)
         for d in range(1, T):
             send(move(gat.at[mine], gat.at[mine], gz_sem, j * (T - 1) + d - 1, (seg, (k + d) % T, s)))
+        if j == last:
+            for d in range(1, Y):
+                for e in range(T):
+                    to = (seg, (k + e) % T, 2 * ((y + d) % Y) + core)
+                    send(move(gat.at[mine], gat.at[mine], gl_sem, (d - 1) * T + e, to))
 
     def gy_start(j):
         for d in range(1, T):
             arrived(gat.at[shard(j, y, (k - d + T) % T)], gz_sem, j * (T - 1) + d - 1)
         mine = band(j, core, y)
-        for d in range(1, Y):
+        for d in range(1, Y if j != last else 1):
             send(move(mine, mine, gy_sem, j * (Y - 1) + d - 1, at_y((y + d) % Y)))
         send(move(mine, mine, gc_sem, j * Y, sibling))
 
     def gc_start(j):
         for d in range(1, Y):
             theirs = band(j, core, (y - d + Y) % Y)
-            arrived(theirs, gy_sem, j * (Y - 1) + d - 1)
+            if j == last:
+                for e in range(T):
+                    piece = gat.at[shard(j, (y - d + Y) % Y, (k - e + T) % T)]
+                    arrived(piece, gl_sem, (d - 1) * T + e)
+            else:
+                arrived(theirs, gy_sem, j * (Y - 1) + d - 1)
             send(move(theirs, theirs, gc_sem, j * Y + d, sibling))
 
     def written(j):
@@ -575,6 +586,7 @@
                 dma((2, count * (T - 1))),
                 dma((2, count * (Y - 1))),
                 dma((2, count * Y)),
+                dma((2, (Y - 1) * T)),
                 dma((10,)),
             ],
             compiler_params=pltpu.CompilerParams(
@@ -589,15 +601,7 @@
             dec_weight.reshape(27, 256, 128),
             out_grad,
         )
-        wide = pl.pallas_call(
-            widen,
-            grid=(6,),
-            out_shape=jax.ShapeDtypeStruct((9 * BLOCK, 128), F32),
-            in_specs=[pl.BlockSpec((9 * BLOCK // 6, 128), lambda i: (i, 0))],
-            out_specs=pl.BlockSpec((9 * BLOCK // 6, 128), lambda i: (i, 0)),
-            cost_estimate=pl.CostEstimate(flops=0, bytes_accessed=54 * BLOCK * 128, transcendentals=0),
-        )(wout)
-        return latp[None], wide.reshape(1, TAPS, 32768)
+        return latp[None], wout.reshape(1, TAPS, 32768).astype(F32)
 
     placed = (P("tm", "space", None, None), P(), P(), P("tm", "space", None, None))
     return jax.shard_map(

time: 70.9 us -> 69.9 us (0.986)
  Pallas kernels: 69.2 us -> 64.8 us
  other arithmetic: 0 us -> 3.54 us
    pallas_call x1 -> x0, Pallas kernels: 4.94 us -> none  [on_device(): pl.pallas_call(widen, grid=(6,), out_shape=jax.ShapeDtypeStruct((9 * BLOC...]
    convert_element_type x0 -> x1, other arithmetic: none -> 3.54 us  [on_device(): return (latp[None], wout.reshape(1, TAPS, 32768).astype(F32))]
where the time goes in v3:
time: 69.9 us; the launch traced here: 69.7 us
  Pallas kernels  64.8 us (93%)
  other arithmetic  3.54 us (5%)
  local copies, waits for them, and re-layouts  0.71 us (1%)
    pallas_call x1, Pallas kernels, on_device(): pl.pallas_call(functools.partial(kernel, T, S, shards, scale), out_shape=...  64.8 us
    convert_element_type x1, other arithmetic, on_device(): return (latp[None], wout.reshape(1, TAPS, 32768).astype(F32))  3.54 us

profile of v3, /device:TPU:1, one launch (start us, length us, event | category | flops | bytes accessed | tf_op | source)
XLA Modules:
  0.0 69.7 jit_solution(15040439792602022758)
XLA Ops:
  0.6 64.8 %shard_map.59 = (bf16[2,4,64,256]{3,2,1,0:T(8,128)(2,1)}, bf16[6912,128]{1,0:T(8,128)(2,1)}) custom-call(bf16[4,8,128,128]{3,2,1,0:T(8,128)(2,1)} %clip.1, bf16[9,384,256]{2,1,0:T(8,128)(2,1)} %bitcast.6, bf16[27,256,128]{2,1,0:T(8,128)(2,1)} %bitcast.7, bf16[2,4,64,128]{3,2,1,0:T(8,128)(2,1)} %og_h.1), custom_call_target="tpu_custom_call" | custom-call | flops 5000000000 | bytes 12000000 | tf_op jit(solution)/shard_map/pallas_call | solution.py:549
  65.4 0.0 copy-start
  65.5 3.5 %convert_element_type.16 = f32[6912,128]{1,0:T(8,128)} convert(bf16[6912,128]{1,0:T(8,128)(2,1)} %get-tuple-element.5) | non-fusion elementwise | flops 884736 | bytes 5308416 | tf_op jit(solution)/shard_map/convert_element_type | solution.py:604
  69.0 0.0 copy-done
  69.0 0.7 %copy.9 = bf16[1,2,4,64,256]{4,3,2,1,0:T(8,128)(2,1)} copy(bf16[1,2,4,64,256]{4,3,2,1,0:T(8,128)(2,1)S(1)} %bitcast.5) | data formatting | bytes 524288
Async XLA Ops:
  65.4 3.6 %copy-start = (bf16[2,4,64,256]{3,2,1,0:T(8,128)(2,1)S(1)}, bf16[2,4,64,256]{3,2,1,0:T(8,128)(2,1)}, u32[]{:S(2)}) copy-start(bf16[2,4,64,256]{3,2,1,0:T(8,128)(2,1)} %get-tuple-element.4) | copy-start | bytes 786436

commit v4 on v3

--- a/solution.py
+++ b/solution.py
@@ -28,7 +28,6 @@
     T,
     S,
     shards,
-    scale,
     clip,
     ew_h,
     dw_h,
@@ -57,6 +56,7 @@
     red2,
     rcvz,
     gat,
+    wide,
     lsem,
     ssem,
     rsem,
@@ -463,7 +463,7 @@
             arrived(rcvz.at[d - 1, off[j] : off[j] + sh[j]], z_sem, j * (T - 1) + d - 1)
             total = total + rcvz[d - 1, off[j] : off[j] + sh[j], :].astype(F32)
         mine = shard(j, y, k)
-        gat[mine, :] = (total * scale).astype(BF)
+        gat[mine, :] = total.astype(BF)
         for d in range(1, T):
             send(move(gat.at[mine], gat.at[mine], gz_sem, j * (T - 1) + d - 1, (seg, (k + d) % T, s)))
         if j == last:
@@ -494,7 +494,7 @@
     def written(j):
         copies = []
         for i, (a, b) in enumerate(CHUNKS[j]):
-            src = gat.at[off[j] * n + i * BLOCK : off[j] * n + (i + 1) * BLOCK]
+            src = wide.at[off[j] * n + i * BLOCK : off[j] * n + (i + 1) * BLOCK]
             dst = wout.at[(3 * a + b) * BLOCK : (3 * a + b + 1) * BLOCK]
             copies.append(pltpu.make_async_copy(src, dst, osem.at[1 + 3 * a + b]))
         return copies
@@ -502,6 +502,8 @@
     def finish(j):
         for d in range(Y):
             arrived(band(j, 1 - core, (y - d + Y) % Y), gc_sem, j * Y + d)
+        used = slice(off[j] * n, off[j] * n + len(CHUNKS[j]) * BLOCK)
+        wide[used, :] = gat[used, :].astype(F32)
         for copy in written(j):
             copy.start()
 
@@ -547,10 +549,10 @@
         scale = 1.0 / math.sqrt(2 * 4 * 64 * n)
         dma = pltpu.SemaphoreType.DMA
         latp, wout = pl.pallas_call(
-            functools.partial(kernel, T, S, shards, scale),
+            functools.partial(kernel, T, S, shards),
             out_shape=(
                 jax.ShapeDtypeStruct((2, 4, 64, 256), BF),
-                jax.ShapeDtypeStruct((9 * BLOCK, 128), BF),
+                jax.ShapeDtypeStruct((9 * BLOCK, 128), F32),
             ),
             in_specs=[pl.BlockSpec(memory_space=pltpu.HBM)] * 4,
             out_specs=(pl.BlockSpec(memory_space=pl.ANY),) * 2,
@@ -577,6 +579,7 @@
                 pltpu.VMEM((T * sh, 128), BF),
                 pltpu.VMEM((T - 1, sh, 128), BF),
                 pltpu.VMEM((n * sh, 128), BF),
+                pltpu.VMEM((n * sh, 128), F32),
                 dma((5,)),
                 dma((24,)),
                 dma((24,)),
@@ -601,7 +604,7 @@
             dec_weight.reshape(27, 256, 128),
             out_grad,
         )
-        return latp[None], wout.reshape(1, TAPS, 32768).astype(F32)
+        return latp[None], (wout * scale).reshape(1, TAPS, 32768)
 
     placed = (P("tm", "space", None, None), P(), P(), P("tm", "space", None, None))
     return jax.shard_map(

time: 69.9 us -> 70.8 us (1.013)
    mul x0 -> x1, other arithmetic: none -> 4.14 us  [on_device(): return (latp[None], (wout * scale).reshape(1, TAPS, 32768))]
    convert_element_type x1 -> x0, other arithmetic: 3.54 us -> none  [on_device(): return (latp[None], wout.reshape(1, TAPS, 32768).astype(F32))]
where the time goes in v4:
time: 70.8 us; the launch traced here: 70.6 us
  Pallas kernels  65.1 us (92%)
  other arithmetic  4.14 us (6%)
  local copies, waits for them, and re-layouts  0.71 us (1%)
    pallas_call x1, Pallas kernels, on_device(): pl.pallas_call(functools.partial(kernel, T, S, shards), out_shape=(jax.Sh...  65.1 us
    mul x1, other arithmetic, on_device(): return (latp[None], (wout * scale).reshape(1, TAPS, 32768))  4.14 us

profile of v4, /device:TPU:1, one launch (start us, length us, event | category | flops | bytes accessed | tf_op | source)
XLA Modules:
  0.0 70.6 jit_solution(1444765251148916084)
XLA Ops:
  0.6 65.1 %shard_map.59 = (bf16[2,4,64,256]{3,2,1,0:T(8,128)(2,1)}, f32[6912,128]{1,0:T(8,128)}) custom-call(bf16[4,8,128,128]{3,2,1,0:T(8,128)(2,1)} %clip.1, bf16[9,384,256]{2,1,0:T(8,128)(2,1)} %bitcast.6, bf16[27,256,128]{2,1,0:T(8,128)(2,1)} %bitcast.7, bf16[2,4,64,128]{3,2,1,0:T(8,128)(2,1)} %og_h.1), custom_call_target="tpu_custom_call" | custom-call | flops 5000000000 | bytes 12000000 | tf_op jit(solution)/shard_map/pallas_call | solution.py:551
  65.8 0.0 copy-start
  65.8 4.1 %broadcast_multiply_fusion = f32[6912,128]{1,0:T(8,128)} fusion(f32[6912,128]{1,0:T(8,128)} %get-tuple-element.5), kind=kLoop, calls=%fused_computation | loop fusion | flops 884736 | bytes 7077888 | tf_op jit(solution)/shard_map/mul | solution.py:607
  69.9 0.0 copy-done
  69.9 0.7 copy.9
Async XLA Ops:
  65.8 4.2 %copy-start = (bf16[2,4,64,256]{3,2,1,0:T(8,128)(2,1)S(1)}, bf16[2,4,64,256]{3,2,1,0:T(8,128)(2,1)}, u32[]{:S(2)}) copy-start(bf16[2,4,64,256]{3,2,1,0:T(8,128)(2,1)} %get-tuple-element.4) | copy-start | bytes 786436
